TPU v7x, 32 devices: a whole 2x2x4 slice. The times are simulated.
32 devices in a mesh: label: 4 (over y, x), batch: 8 (over z, core).
Axes of the slice: x: 2, y: 2, z: 4, core: 2. Of those that a mesh axis runs over, the one named last changes fastest.
Arguments:
- queries: bfloat16 [4096, 768], P('batch'), may hold values from -6 to 6
- slab: bfloat16 [51200, 768], P(('label', 'batch')), may hold values from -0.21875 to 0.21875
- positives: int32 [4096, 51200], P('batch', 'label'), may hold values 0 or 1
Outputs:
- query_grad: bfloat16 [4096, 768], P('batch')
- slab_grad: bfloat16 [51200, 768], P(('label', 'batch'))
All inputs are finite; a program needn't handle non-finite values. No bound on the sum of `positives` on one device may be relied on, other than what follows from the above.
Results may differ from a plain program's by a relative error of at most 0.0037.
Values may be sent and summed in bfloat16 or wider, within the bound.
A program may use at most 192 MiB of HBM per device.

v0:
```python
import jax
import jax.numpy as jnp
from jax import lax
from jax.experimental import pallas as pl
from jax.experimental.pallas import tpu as pltpu
from jax.sharding import PartitionSpec as P

loss_weight = 0.0625
MESH = pl.DeviceIdType.MESH
F32, BF16 = jnp.float32, jnp.bfloat16
PARTS = 5


def plain(queries, slab, positives):
    piece = lax.all_gather(slab, "batch", axis=0, tiled=True)
    logits = lax.dot_general(queries, piece, (((1,), (1,)), ((), ())), preferred_element_type=F32)
    grad = ((jax.nn.sigmoid(logits) - positives.astype(F32)) * loss_weight).astype(BF16)
    query_grad = lax.psum(jnp.dot(grad, piece, preferred_element_type=F32), "label").astype(BF16)
    slab_grad = lax.psum_scatter(
        lax.dot_general(grad, queries, (((0,), (0,)), ((), ())), preferred_element_type=F32),
        "batch",
        scatter_dimension=0,
        tiled=True,
    ).astype(BF16)
    return query_grad, slab_grad


def remote(src, dst, send, recv, device):
    return pltpu.make_async_remote_copy(
        src_ref=src, dst_ref=dst, send_sem=send, recv_sem=recv, device_id=device, device_id_type=MESH
    )


def line_kernel(
    n, win,
    q_ref, slab_ref, pos_ref,
    qout, sout, posin,
    G, RS, PS, qb, qacc, pt, gs, qr, xr,
    loc_sem, q_send, q_recv, p_send, p_recv, pt_sem, g_send, g_recv, r_send, r_recv, a_send, a_recv, x_send, x_recv,
):
    K, w, D = slab_ref.shape
    rows = q_ref.shape[0]
    half = rows // 2
    l = lax.axis_index("label")
    b = lax.axis_index("batch")
    z, c = b // 2, b % 2
    zm = n - 1 - z
    sib = {"batch": b + 1 - 2 * c}
    right, left = {"batch": b + 2}, {"batch": b - 2}
    partner = ({"label": l + 1 - 2 * (l % 2)}, {"label": l + 2 - 4 * (l // 2)})
    has_r, has_l = z < n - 1, z > 0

    barrier = pltpu.get_barrier_semaphore()
    for dev in (sib, *partner):
        pl.semaphore_signal(barrier, inc=1, device_id=dev, device_id_type=MESH)

    @pl.when(has_r)
    def _():
        pl.semaphore_signal(barrier, inc=1, device_id=right, device_id_type=MESH)

    @pl.when(has_l)
    def _():
        pl.semaphore_signal(barrier, inc=1, device_id=left, device_id_type=MESH)

    pl.semaphore_wait(barrier, 3 + has_r.astype(jnp.int32) + has_l.astype(jnp.int32))

    def column(block, core, k):
        return pl.multiple_of(block * (2 * K * w) + core * (K * w) + k * w - 64 * ((k + core) % 2), 128)

    def own_right(k):
        return remote(slab_ref.at[k], G.at[z, k], g_send.at[0, z, k], g_recv.at[z, k], right)

    def own_left(k):
        return remote(slab_ref.at[k], G.at[z, k], g_send.at[1, z, k], g_recv.at[z, k], left)

    def pass_right(block, k):
        return remote(G.at[block, k], G.at[block, k], g_send.at[0, block, k], g_recv.at[block, k], right)

    def pass_left(block, k):
        return remote(G.at[block, k], G.at[block, k], g_send.at[1, block, k], g_recv.at[block, k], left)

    def swap(block, k):
        return remote(
            pos_ref.at[:, pl.ds(column(block, 1 - c, k), win)], posin.at[block, k],
            p_send.at[block, k], p_recv.at[block, k], sib,
        )

    def send_q():
        return remote(q_ref, qb.at[1], q_send, q_recv, sib)

    def local_slab(k):
        return pltpu.make_async_copy(slab_ref.at[k], G.at[z, k], loc_sem.at[k])

    def sum_right(dest, k):
        return remote(RS.at[dest, k], RS.at[dest, k], r_send.at[dest, k], r_recv.at[dest, k], right)

    def sum_left(dest, k):
        slot = jnp.where(dest == z - 1, n, dest)
        return remote(RS.at[dest, k], RS.at[slot, k], r_send.at[dest, k], r_recv.at[slot, k], left)

    def arrived(slot, k):
        remote(RS.at[slot, k], RS.at[slot, k], r_send.at[0, 0], r_recv.at[slot, k], sib).wait_recv()

    q_own = pltpu.make_async_copy(q_ref, qb.at[0], loc_sem.at[K])
    q_own.start()
    send_q().start()

    @pl.loop(0, K)
    def _(k):
        @pl.when(has_r)
        def _():
            own_right(k).start()

        @pl.when(has_l)
        def _():
            own_left(k).start()

        local_slab(k).start()
        swap(z, k).start()

    @pl.loop(0, (n - 1) * K)
    def _(j):
        d, k = j // K + 1, j % K

        @pl.when(z + d < n)
        def _():
            swap(z + d, k).start()

        @pl.when(z - d >= 0)
        def _():
            swap(z - d, k).start()

    qacc[...] = jnp.zeros_like(qacc)
    q_own.wait()
    send_q().wait_recv()

    def tile(block, k):
        swap(block, k).wait_recv()
        mine = pltpu.make_async_copy(pos_ref.at[:, pl.ds(column(block, c, k), win)], pt.at[0], pt_sem.at[0])
        theirs = pltpu.make_async_copy(posin.at[block, k], pt.at[1], pt_sem.at[1])
        mine.start()
        theirs.start()
        mine.wait()
        theirs.wait()
        odd = (k + c) % 2 == 1

        @pl.loop(0, 2)
        def _(h):
            labels = G[block, k]
            logits = lax.dot_general(qb[h], labels, (((1,), (1,)), ((), ())), preferred_element_type=F32)
            marks = jnp.where(odd, pt[h, :, 64 : 64 + w], pt[h, :, 0:w]).astype(F32)
            grad = ((jax.nn.sigmoid(logits) - marks) * loss_weight).astype(BF16)
            gs[h] = grad
            qacc[h] += jnp.dot(grad, labels, preferred_element_type=F32)

        grads = gs[...].reshape(2 * rows, w)
        both = qb[...].reshape(2 * rows, D)
        PS[block, k] = lax.dot_general(grads, both, (((0,), (0,)), ((), ())), preferred_element_type=F32)

    def turn(j, at, s):
        third = j - 2 * K - at
        second = jnp.where(at == 0, j - K, jnp.where(j - 2 * K < 2, j - 2 * K, j - 3 * K + 1))
        second_ok = (at == 0) | ((at == 1) & ((j - 2 * K < 2) | (second >= 2)))
        first = jnp.where(j == K - 1, 0, j - 3 * K + 2)
        first_ok = (at == 0) & ((j == K - 1) | (first >= 1))
        k = jnp.where(s == 0, second, jnp.where(s == 1, third, first))
        far = jnp.where(s == 0, 2, jnp.where(s == 1, 3, 1))
        ok = jnp.where(s == 0, second_ok, jnp.where(s == 1, at < 3, first_ok))
        return far, k, ok & (k >= 0) & (k < K)

    def sums(j):
        for at, going_right in ((z, True), (zm, False)):

            @pl.loop(0, 3)
            def _(s, at=at, going_right=going_right):
                far, k, ok = turn(j, at, s)
                dest = far if going_right else n - 1 - far

                @pl.when(ok)
                def _():
                    @pl.when(at > 0)
                    def _():
                        arrived(dest, k)
                        RS[dest, k] = (RS[dest, k].astype(F32) + PS[dest, k]).astype(BF16)

                    @pl.when(at == 0)
                    def _():
                        RS[dest, k] = PS[dest, k].astype(BF16)

                    (sum_right if going_right else sum_left)(dest, k).start()

        t = j - 3 * K - 2

        @pl.when((t >= 0) & (t < K))
        def _():
            @pl.when(has_l)
            def _():
                arrived(z, t)
                PS[z, t] += RS[z, t].astype(F32)

            @pl.when(has_r)
            def _():
                arrived(n, t)
                PS[z, t] += RS[n, t].astype(F32)

            sout[t] = PS[z, t].astype(BF16)

    @pl.loop(0, (n - 1) * K)
    def _(j):
        d, k = j // K + 1, j % K

        @pl.when(j < K)
        def _():
            local_slab(k).wait()

        @pl.loop(0, 3)
        def _(s):
            block = jnp.where(s == 0, z, jnp.where(s == 1, z + d, z - d))

            @pl.when((s == 1) & (block < n))
            def _():
                pass_left(block, k).wait_recv()

                @pl.when(has_l)
                def _():
                    pass_left(block, k).start()

            @pl.when((s == 2) & (block >= 0))
            def _():
                pass_right(block, k).wait_recv()

                @pl.when(has_r)
                def _():
                    pass_right(block, k).start()

            @pl.when(((s == 0) & (j < K)) | ((s > 0) & (block >= 0) & (block < n)))
            def _():
                tile(block, k)

        sums(j)

    theirs = remote(qacc.at[1], qr, a_send, a_recv, sib)
    theirs.start()
    theirs.wait_recv()
    qacc[0] += qr[...]

    def over(stage, h):
        src = qacc.at[0, pl.ds(h * half, half)] if stage == 0 else xr.at[0, h]
        dev = partner[h] if stage == 0 else partner[1 - h]
        return remote(src, xr.at[stage, h], x_send.at[stage, h], x_recv.at[stage, h], dev)

    for h in range(2):
        over(0, h).start()

    first, mid, last = (n - 1) * K, (n - 1) * K + 2, n * K + 2
    pl.loop(first, mid)(sums)
    for h in range(2):
        over(0, h).wait_recv()
        xr[0, h] += qacc[0, h * half : (h + 1) * half, :]
        over(1, h).start()
    pl.loop(mid, last)(sums)
    for h in range(2):
        over(1, h).wait_recv()
        qout[h * half : (h + 1) * half, :] = (xr[0, h] + xr[1, h]).astype(BF16)

    for h in range(2):
        over(0, h).wait_send()
        over(1, h).wait_send()
    theirs.wait_send()
    send_q().wait_send()

    @pl.loop(0, n * K)
    def _(j):
        block, k = j // K, j % K
        swap(block, k).wait_send()

        @pl.when(has_r & (block <= z))
        def _():
            pass_right(block, k).wait_send()

        @pl.when(has_l & (block >= z))
        def _():
            pass_left(block, k).wait_send()

        @pl.when(block != z)
        def _():
            sum_right(block, k).wait_send()


def copy_kernel(q_ref, s_ref, q_out, s_out, q_vmem, s_vmem, sem):
    K, rows = s_ref.shape[0], q_ref.shape[0] // 2
    parts = [(s_ref.at[k], s_vmem.at[k], s_out.at[k]) for k in range(K)]
    for h in range(2):
        part = pl.ds(h * rows, rows)
        parts.append((q_ref.at[part], q_vmem.at[part], q_out.at[part]))
    come = [pltpu.make_async_copy(src, mid, sem.at[0, i]) for i, (src, mid, _) in enumerate(parts)]
    go = [pltpu.make_async_copy(mid, dst, sem.at[1, i]) for i, (_, mid, dst) in enumerate(parts)]
    for copy in come:
        copy.start()
    for before, after in zip(come, go):
        before.wait()
        after.start()
    for copy in go:
        copy.wait()


def hand_over(query_grad, slab_grad):
    hbm = pl.BlockSpec(memory_space=pl.ANY)
    return pl.pallas_call(
        copy_kernel,
        out_shape=tuple(jax.ShapeDtypeStruct(x.shape, x.dtype) for x in (query_grad, slab_grad)),
        in_specs=[hbm, hbm],
        out_specs=(hbm, hbm),
        scratch_shapes=[
            pltpu.VMEM(query_grad.shape, query_grad.dtype),
            pltpu.VMEM(slab_grad.shape, slab_grad.dtype),
            pltpu.SemaphoreType.DMA((2, slab_grad.shape[0] + 2)),
        ],
    )(query_grad, slab_grad)


def fused(n, queries, slab, positives):
    rows, D = queries.shape
    R = slab.shape[0]
    K, w = PARTS, R // PARTS
    win = w + 64
    vmem = pl.BlockSpec(memory_space=pltpu.VMEM)
    hbm = pl.BlockSpec(memory_space=pl.ANY)
    dma = pltpu.SemaphoreType.DMA
    query_grad, slab_grad, _ = pl.pallas_call(
        lambda *refs: line_kernel(n, win, *refs),
        out_shape=(
            jax.ShapeDtypeStruct((rows, D), BF16),
            jax.ShapeDtypeStruct((K, w, D), BF16),
            jax.ShapeDtypeStruct((n, K, rows, win), jnp.int32),
        ),
        in_specs=[hbm, hbm, hbm],
        out_specs=(vmem, vmem, hbm),
        scratch_shapes=[
            pltpu.VMEM((n, K, w, D), BF16),
            pltpu.VMEM((n + 1, K, w, D), BF16),
            pltpu.VMEM((n, K, w, D), F32),
            pltpu.VMEM((2, rows, D), BF16),
            pltpu.VMEM((2, rows, D), F32),
            pltpu.VMEM((2, rows, win), jnp.int32),
            pltpu.VMEM((2, rows, w), BF16),
            pltpu.VMEM((rows, D), F32),
            pltpu.VMEM((2, 2, rows // 2, D), F32),
            dma((K + 1,)), dma, dma, dma((n, K)), dma((n, K)), dma((2,)),
            dma((2, n, K)), dma((n, K)), dma((n, K)), dma((n + 1, K)), dma, dma, dma((2, 2)), dma((2, 2)),
        ],
        compiler_params=pltpu.CompilerParams(
            collective_id=0, has_side_effects=True, vmem_limit_bytes=62 * 2**20
        ),
        cost_estimate=pl.CostEstimate(
            flops=12 * rows * n * R * D, bytes_accessed=rows * n * R * 8, transcendentals=2 * rows * n * R
        ),
    )(queries, slab.reshape(K, w, D), positives)
    query_grad, slab_grad = hand_over(query_grad, slab_grad)
    return query_grad, slab_grad.reshape(R, D)


def solution(mesh):
    labels, batch = mesh.shape["label"], mesh.shape["batch"]

    def per_device(queries, slab, positives):
        R = slab.shape[0]
        fits = labels == 4 and batch == 8 and R % (PARTS * 64) == 0 and (R // PARTS) % 128 == 64
        if fits and (R // 64) % 2 == 1 and queries.shape[0] % 32 == 0 and R <= 1600:
            return fused(batch // 2, queries, slab, positives)
        return plain(queries, slab, positives)

    return jax.shard_map(
        per_device,
        mesh=mesh,
        in_specs=(P("batch", None), P(("label", "batch"), None), P("batch", "label")),
        out_specs=(P("batch", None), P(("label", "batch"), None)),
        check_vma=False,
    )
```

profile of v0, /device:TPU:0, one launch (start us, length us, event | category | flops | bytes accessed | tf_op | source)
XLA Modules:
  0.0 226.7 jit_solution(5093293118642399563)
XLA Ops:
  0.6 223.2 %shard_map.50 = (bf16[512,768]{1,0:T(8,128)(2,1)}, bf16[5,320,768]{2,1,0:T(8,128)(2,1)}, s32[4,5,512,384]{3,2,1,0:T(8,128)}) custom-call(bf16[512,768]{1,0:T(8,128)(2,1)} %refs_0_.1, bf16[5,320,768]{2,1,0:T(8,128)(2,1)} %bitcast.2, s32[512,12800]{1,0:T(8,128)} %refs_2_.1), custom_call_target="tpu_custom_call" | custom-call | flops 30198988800 | bytes 26214400 | tf_op jit(solution)/shard_map/pallas_call | solution.py:330
  223.8 2.8 %shard_map.51 = (bf16[512,768]{1,0:T(8,128)(2,1)}, bf16[5,320,768]{2,1,0:T(8,128)(2,1)}) custom-call(bf16[512,768]{1,0:T(8,128)(2,1)} %get-tuple-element.6.q_ref, bf16[5,320,768]{2,1,0:T(8,128)(2,1)} %get-tuple-element.7.s_ref), custom_call_target="tpu_custom_call" | custom-call | tf_op jit(solution)/shard_map/pallas_call | solution.py:309
where the time goes:
time: 229 us; the launch traced here: 227 us
  Pallas kernels  226 us (99%)
    pallas_call x1, Pallas kernels, fused(): pl.pallas_call(lambda *refs: line_kernel(n, win, *refs), out_shape=(jax.S...  223 us

commit v1 on v0

--- a/solution.py
+++ b/solution.py
@@ -9,6 +9,7 @@
 MESH = pl.DeviceIdType.MESH
 F32, BF16 = jnp.float32, jnp.bfloat16
 PARTS = 5
+NEAR, MID = 4, 7
 
 
 def plain(queries, slab, positives):
@@ -39,6 +40,7 @@
     loc_sem, q_send, q_recv, p_send, p_recv, pt_sem, g_send, g_recv, r_send, r_recv, a_send, a_recv, x_send, x_recv,
 ):
     K, w, D = slab_ref.shape
+    H = 2 * K
     rows = q_ref.shape[0]
     half = rows // 2
     l = lax.axis_index("label")
@@ -62,6 +64,17 @@
     def _():
         pl.semaphore_signal(barrier, inc=1, device_id=left, device_id_type=MESH)
 
+    def local_slab(k):
+        return pltpu.make_async_copy(slab_ref.at[k], G.at[z, k], loc_sem.at[k])
+
+    q_own = pltpu.make_async_copy(q_ref, qb.at[0], loc_sem.at[K])
+    q_own.start()
+
+    @pl.loop(0, K)
+    def _(k):
+        local_slab(k).start()
+
+    qacc[...] = jnp.zeros_like(qacc)
     pl.semaphore_wait(barrier, 3 + has_r.astype(jnp.int32) + has_l.astype(jnp.int32))
 
     def column(block, core, k):
@@ -88,22 +101,15 @@
     def send_q():
         return remote(q_ref, qb.at[1], q_send, q_recv, sib)
 
-    def local_slab(k):
-        return pltpu.make_async_copy(slab_ref.at[k], G.at[z, k], loc_sem.at[k])
-
-    def sum_right(dest, k):
-        return remote(RS.at[dest, k], RS.at[dest, k], r_send.at[dest, k], r_recv.at[dest, k], right)
-
-    def sum_left(dest, k):
+    def sum_right(dest, h):
+        return remote(RS.at[dest, h], RS.at[dest, h], r_send.at[dest, h], r_recv.at[dest, h], right)
+
+    def sum_left(dest, h):
         slot = jnp.where(dest == z - 1, n, dest)
-        return remote(RS.at[dest, k], RS.at[slot, k], r_send.at[dest, k], r_recv.at[slot, k], left)
-
-    def arrived(slot, k):
-        remote(RS.at[slot, k], RS.at[slot, k], r_send.at[0, 0], r_recv.at[slot, k], sib).wait_recv()
-
-    q_own = pltpu.make_async_copy(q_ref, qb.at[0], loc_sem.at[K])
-    q_own.start()
-    send_q().start()
+        return remote(RS.at[dest, h], RS.at[slot, h], r_send.at[dest, h], r_recv.at[slot, h], left)
+
+    def arrived(slot, h):
+        remote(RS.at[slot, h], RS.at[slot, h], r_send.at[0, 0], r_recv.at[slot, h], sib).wait_recv()
 
     @pl.loop(0, K)
     def _(k):
@@ -115,7 +121,10 @@
         def _():
             own_left(k).start()
 
-        local_slab(k).start()
+        @pl.when(k == 0)
+        def _():
+            send_q().start()
+
         swap(z, k).start()
 
     @pl.loop(0, (n - 1) * K)
@@ -130,18 +139,23 @@
         def _():
             swap(z - d, k).start()
 
-    qacc[...] = jnp.zeros_like(qacc)
     q_own.wait()
     send_q().wait_recv()
 
-    def tile(block, k):
-        swap(block, k).wait_recv()
+    def marks_of(block, k):
         mine = pltpu.make_async_copy(pos_ref.at[:, pl.ds(column(block, c, k), win)], pt.at[0], pt_sem.at[0])
         theirs = pltpu.make_async_copy(posin.at[block, k], pt.at[1], pt_sem.at[1])
+        return mine, theirs
+
+    def fetch(block, k):
+        mine, theirs = marks_of(block, k)
         mine.start()
+        swap(block, k).wait_recv()
         theirs.start()
-        mine.wait()
-        theirs.wait()
+
+    def tile(block, k):
+        for copy in marks_of(block, k):
+            copy.wait()
         odd = (k + c) % 2 == 1
 
         @pl.loop(0, 2)
@@ -155,43 +169,45 @@
 
         grads = gs[...].reshape(2 * rows, w)
         both = qb[...].reshape(2 * rows, D)
-        PS[block, k] = lax.dot_general(grads, both, (((0,), (0,)), ((), ())), preferred_element_type=F32)
-
-    def turn(j, at, s):
-        third = j - 2 * K - at
-        second = jnp.where(at == 0, j - K, jnp.where(j - 2 * K < 2, j - 2 * K, j - 3 * K + 1))
-        second_ok = (at == 0) | ((at == 1) & ((j - 2 * K < 2) | (second >= 2)))
-        first = jnp.where(j == K - 1, 0, j - 3 * K + 2)
-        first_ok = (at == 0) & ((j == K - 1) | (first >= 1))
-        k = jnp.where(s == 0, second, jnp.where(s == 1, third, first))
-        far = jnp.where(s == 0, 2, jnp.where(s == 1, 3, 1))
-        ok = jnp.where(s == 0, second_ok, jnp.where(s == 1, at < 3, first_ok))
-        return far, k, ok & (k >= 0) & (k < K)
-
-    def sums(j):
+        part = lax.dot_general(grads, both, (((0,), (0,)), ((), ())), preferred_element_type=F32)
+        PS[block, pl.ds(2 * k, 2)] = part.reshape(2, w // 2, D)
+
+    def turn(i, at):
+        near_far = jnp.where(i < H, 1, jnp.where(i < 2 * H, 2, jnp.where(i < 3 * H, 3, 1)))
+        near_h = i - jnp.where(i < H, H - NEAR, jnp.where(i < 2 * H, H, jnp.where(i < 3 * H, 2 * H, 3 * H - NEAR)))
+        near_ok = (i >= H - NEAR) & (i < 4 * H - NEAR)
+        m = i - NEAR
+        mid_far = jnp.where((m >= 2 * H) & (m < 3 * H), 3, 2)
+        mid_h = m - jnp.where(m < 2 * H, H, jnp.where(m < 3 * H, 2 * H, 3 * H - MID))
+        mid_ok = (m >= H) & ((m < H + MID) | (m >= 2 * H)) & (m < 4 * H - MID)
+        last_h = i - 2 * H - MID
+        last_ok = (last_h >= 0) & (last_h < H)
+        far = jnp.where(at == 0, near_far, jnp.where(at == 1, mid_far, 3))
+        h = jnp.where(at == 0, near_h, jnp.where(at == 1, mid_h, last_h))
+        ok = ((at == 0) & near_ok) | ((at == 1) & mid_ok) | ((at == 2) & last_ok)
+        return far, h, ok
+
+    def sums(i):
         for at, going_right in ((z, True), (zm, False)):
-
-            @pl.loop(0, 3)
-            def _(s, at=at, going_right=going_right):
-                far, k, ok = turn(j, at, s)
-                dest = far if going_right else n - 1 - far
-
-                @pl.when(ok)
+            far, h, ok = turn(i, at)
+            dest = far if going_right else n - 1 - far
+
+            @pl.when(ok)
+            def _(at=at, h=h, dest=dest, going_right=going_right):
+                @pl.when(at > 0)
                 def _():
-                    @pl.when(at > 0)
-                    def _():
-                        arrived(dest, k)
-                        RS[dest, k] = (RS[dest, k].astype(F32) + PS[dest, k]).astype(BF16)
-
-                    @pl.when(at == 0)
-                    def _():
-                        RS[dest, k] = PS[dest, k].astype(BF16)
-
-                    (sum_right if going_right else sum_left)(dest, k).start()
-
-        t = j - 3 * K - 2
-
-        @pl.when((t >= 0) & (t < K))
+                    arrived(dest, h)
+                    RS[dest, h] = (RS[dest, h].astype(F32) + PS[dest, h]).astype(BF16)
+
+                @pl.when(at == 0)
+                def _():
+                    RS[dest, h] = PS[dest, h].astype(BF16)
+
+                (sum_right if going_right else sum_left)(dest, h).start()
+
+        t = i - 3 * H
+
+        @pl.when((t >= 0) & (t < H))
         def _():
             @pl.when(has_l)
             def _():
@@ -216,6 +232,11 @@
         @pl.loop(0, 3)
         def _(s):
             block = jnp.where(s == 0, z, jnp.where(s == 1, z + d, z - d))
+            busy = ((s == 0) & (j < K)) | ((s > 0) & (block >= 0) & (block < n))
+
+            @pl.when(busy)
+            def _():
+                fetch(block, k)
 
             @pl.when((s == 1) & (block < n))
             def _():
@@ -233,35 +254,37 @@
                 def _():
                     pass_right(block, k).start()
 
-            @pl.when(((s == 0) & (j < K)) | ((s > 0) & (block >= 0) & (block < n)))
+            @pl.when(busy)
             def _():
                 tile(block, k)
 
-        sums(j)
+        @pl.loop(2 * j, 2 * j + 2)
+        def _(i):
+            sums(i)
 
     theirs = remote(qacc.at[1], qr, a_send, a_recv, sib)
-    theirs.start()
-    theirs.wait_recv()
-    qacc[0] += qr[...]
 
     def over(stage, h):
         src = qacc.at[0, pl.ds(h * half, half)] if stage == 0 else xr.at[0, h]
         dev = partner[h] if stage == 0 else partner[1 - h]
         return remote(src, xr.at[stage, h], x_send.at[stage, h], x_recv.at[stage, h], dev)
 
+    theirs.start()
+    pl.loop(3 * H, 3 * H + 1)(sums)
+    theirs.wait_recv()
+    qacc[0] += qr[...]
     for h in range(2):
         over(0, h).start()
-
-    first, mid, last = (n - 1) * K, (n - 1) * K + 2, n * K + 2
-    pl.loop(first, mid)(sums)
+    pl.loop(3 * H + 1, 3 * H + H // 2)(sums)
     for h in range(2):
         over(0, h).wait_recv()
         xr[0, h] += qacc[0, h * half : (h + 1) * half, :]
         over(1, h).start()
-    pl.loop(mid, last)(sums)
+    pl.loop(3 * H + H // 2, 4 * H - 1)(sums)
     for h in range(2):
         over(1, h).wait_recv()
         qout[h * half : (h + 1) * half, :] = (xr[0, h] + xr[1, h]).astype(BF16)
+    pl.loop(4 * H - 1, 4 * H)(sums)
 
     for h in range(2):
         over(0, h).wait_send()
@@ -284,7 +307,8 @@
 
         @pl.when(block != z)
         def _():
-            sum_right(block, k).wait_send()
+            sum_right(block, 2 * k).wait_send()
+            sum_right(block, 2 * k + 1).wait_send()
 
 
 def copy_kernel(q_ref, s_ref, q_out, s_out, q_vmem, s_vmem, sem):
@@ -331,15 +355,15 @@
         lambda *refs: line_kernel(n, win, *refs),
         out_shape=(
             jax.ShapeDtypeStruct((rows, D), BF16),
-            jax.ShapeDtypeStruct((K, w, D), BF16),
+            jax.ShapeDtypeStruct((2 * K, w // 2, D), BF16),
             jax.ShapeDtypeStruct((n, K, rows, win), jnp.int32),
         ),
         in_specs=[hbm, hbm, hbm],
         out_specs=(vmem, vmem, hbm),
         scratch_shapes=[
             pltpu.VMEM((n, K, w, D), BF16),
-            pltpu.VMEM((n + 1, K, w, D), BF16),
-            pltpu.VMEM((n, K, w, D), F32),
+            pltpu.VMEM((n + 1, 2 * K, w // 2, D), BF16),
+            pltpu.VMEM((n, 2 * K, w // 2, D), F32),
             pltpu.VMEM((2, rows, D), BF16),
             pltpu.VMEM((2, rows, D), F32),
             pltpu.VMEM((2, rows, win), jnp.int32),
@@ -347,7 +371,7 @@
             pltpu.VMEM((rows, D), F32),
             pltpu.VMEM((2, 2, rows // 2, D), F32),
             dma((K + 1,)), dma, dma, dma((n, K)), dma((n, K)), dma((2,)),
-            dma((2, n, K)), dma((n, K)), dma((n, K)), dma((n + 1, K)), dma, dma, dma((2, 2)), dma((2, 2)),
+            dma((2, n, K)), dma((n, K)), dma((n, 2 * K)), dma((n + 1, 2 * K)), dma, dma, dma((2, 2)), dma((2, 2)),
         ],
         compiler_params=pltpu.CompilerParams(
             collective_id=0, has_side_effects=True, vmem_limit_bytes=62 * 2**20

time: 229 us -> 225 us (0.983)
    pallas_call x1, Pallas kernels: 223 us -> 220 us  [fused(): pl.pallas_call(lambda *refs: line_kernel(n, win, *refs), out_shape=(jax.S...]
where the time goes in v1:
time: 225 us; the launch traced here: 224 us
  Pallas kernels  224 us (100%)
    pallas_call x1, Pallas kernels, fused(): pl.pallas_call(lambda *refs: line_kernel(n, win, *refs), out_shape=(jax.S...  220 us

profile of v1, /device:TPU:0, one launch (start us, length us, event | category | flops | bytes accessed | tf_op | source)
XLA Modules:
  0.0 224.2 jit_solution(1379319843668127973)
XLA Ops:
  0.6 220.2 %shard_map.50 = (bf16[512,768]{1,0:T(8,128)(2,1)}, bf16[10,160,768]{2,1,0:T(8,128)(2,1)}, s32[4,5,512,384]{3,2,1,0:T(8,128)}) custom-call(bf16[512,768]{1,0:T(8,128)(2,1)} %refs_0_.1, bf16[5,320,768]{2,1,0:T(8,128)(2,1)} %bitcast.2, s32[512,12800]{1,0:T(8,128)} %refs_2_.1), custom_call_target="tpu_custom_call" | custom-call | flops 30198988800 | bytes 26214400 | tf_op jit(solution)/shard_map/pallas_call | solution.py:354
  220.9 3.3 %shard_map.51 = (bf16[512,768]{1,0:T(8,128)(2,1)}, bf16[10,160,768]{2,1,0:T(8,128)(2,1)}) custom-call(bf16[512,768]{1,0:T(8,128)(2,1)} %get-tuple-element.6.q_ref, bf16[10,160,768]{2,1,0:T(8,128)(2,1)} %get-tuple-element.7.s_ref), custom_call_target="tpu_custom_call" | custom-call | tf_op jit(solution)/shard_map/pallas_call | solution.py:333

commit v2 on v1

--- a/solution.py
+++ b/solution.py
@@ -311,36 +311,25 @@
             sum_right(block, 2 * k + 1).wait_send()
 
 
-def copy_kernel(q_ref, s_ref, q_out, s_out, q_vmem, s_vmem, sem):
-    K, rows = s_ref.shape[0], q_ref.shape[0] // 2
-    parts = [(s_ref.at[k], s_vmem.at[k], s_out.at[k]) for k in range(K)]
-    for h in range(2):
-        part = pl.ds(h * rows, rows)
-        parts.append((q_ref.at[part], q_vmem.at[part], q_out.at[part]))
-    come = [pltpu.make_async_copy(src, mid, sem.at[0, i]) for i, (src, mid, _) in enumerate(parts)]
-    go = [pltpu.make_async_copy(mid, dst, sem.at[1, i]) for i, (_, mid, dst) in enumerate(parts)]
-    for copy in come:
+def copy_kernel(q_ref, s_ref, q_out, s_out, sem):
+    copies = [pltpu.make_async_copy(q_ref, q_out, sem.at[0]), pltpu.make_async_copy(s_ref, s_out, sem.at[1])]
+    for copy in copies:
         copy.start()
-    for before, after in zip(come, go):
-        before.wait()
-        after.start()
-    for copy in go:
+    for copy in copies:
         copy.wait()
 
 
 def hand_over(query_grad, slab_grad):
+    vmem = pl.BlockSpec(memory_space=pltpu.VMEM)
     hbm = pl.BlockSpec(memory_space=pl.ANY)
     return pl.pallas_call(
         copy_kernel,
         out_shape=tuple(jax.ShapeDtypeStruct(x.shape, x.dtype) for x in (query_grad, slab_grad)),
-        in_specs=[hbm, hbm],
+        in_specs=[vmem, vmem],
+        compiler_params=pltpu.CompilerParams(vmem_limit_bytes=2**20),
         out_specs=(hbm, hbm),
-        scratch_shapes=[
-            pltpu.VMEM(query_grad.shape, query_grad.dtype),
-            pltpu.VMEM(slab_grad.shape, slab_grad.dtype),
-            pltpu.SemaphoreType.DMA((2, slab_grad.shape[0] + 2)),
-        ],
-    )(query_grad, slab_grad)
+        scratch_shapes=[pltpu.SemaphoreType.DMA((2,))],
+    )(*(pltpu.with_memory_space_constraint(x, pltpu.VMEM) for x in (query_grad, slab_grad)))
 
 
 def fused(n, queries, slab, positives):
@@ -354,8 +343,8 @@
     query_grad, slab_grad, _ = pl.pallas_call(
         lambda *refs: line_kernel(n, win, *refs),
         out_shape=(
-            jax.ShapeDtypeStruct((rows, D), BF16),
-            jax.ShapeDtypeStruct((2 * K, w // 2, D), BF16),
+            pltpu.VMEM((rows, D), BF16),
+            pltpu.VMEM((2 * K, w // 2, D), BF16),
             jax.ShapeDtypeStruct((n, K, rows, win), jnp.int32),
         ),
         in_specs=[hbm, hbm, hbm],
@@ -374,7 +363,7 @@
             dma((2, n, K)), dma((n, K)), dma((n, 2 * K)), dma((n + 1, 2 * K)), dma, dma, dma((2, 2)), dma((2, 2)),
         ],
         compiler_params=pltpu.CompilerParams(
-            collective_id=0, has_side_effects=True, vmem_limit_bytes=62 * 2**20
+            collective_id=0, has_side_effects=True, vmem_limit_bytes=58 * 2**20
         ),
         cost_estimate=pl.CostEstimate(
             flops=12 * rows * n * R * D, bytes_accessed=rows * n * R * 8, transcendentals=2 * rows * n * R

time: 225 us -> 221 us (0.982)
  Pallas kernels: 224 us -> 220 us
where the time goes in v2:
time: 221 us
  Pallas kernels  220 us (100%)
    pallas_call x1, Pallas kernels, fused(): pl.pallas_call(lambda *refs: line_kernel(n, win, *refs), out_shape=(pltpu...  219 us

profile of v2, /device:TPU:0, one launch (start us, length us, event | category | flops | bytes accessed | tf_op | source)
XLA Modules:
  0.0 220.9 jit_solution(9764544386412392792)
XLA Ops:
  0.6 218.5 %shard_map.50 = (bf16[512,768]{1,0:T(8,128)(2,1)S(1)}, bf16[10,160,768]{2,1,0:T(8,128)(2,1)S(1)}, s32[4,5,512,384]{3,2,1,0:T(8,128)}) custom-call(bf16[512,768]{1,0:T(8,128)(2,1)} %refs_0_.1, bf16[5,320,768]{2,1,0:T(8,128)(2,1)} %bitcast.2, s32[512,12800]{1,0:T(8,128)} %refs_2_.1), custom_call_target="tpu_custom_call" | custom-call | flops 30198988800 | bytes 26214400 | tf_op jit(solution)/shard_map/pallas_call | solution.py:343
  219.2 1.7 shard_map.51

commit v3 on v2

--- a/solution.py
+++ b/solution.py
@@ -9,7 +9,7 @@
 MESH = pl.DeviceIdType.MESH
 F32, BF16 = jnp.float32, jnp.bfloat16
 PARTS = 5
-NEAR, MID = 4, 7
+NEAR, MID, LAG = 2, 3, 5
 
 
 def plain(queries, slab, positives):
@@ -40,7 +40,7 @@
     loc_sem, q_send, q_recv, p_send, p_recv, pt_sem, g_send, g_recv, r_send, r_recv, a_send, a_recv, x_send, x_recv,
 ):
     K, w, D = slab_ref.shape
-    H = 2 * K
+    H = K
     rows = q_ref.shape[0]
     half = rows // 2
     l = lax.axis_index("label")
@@ -67,14 +67,6 @@
     def local_slab(k):
         return pltpu.make_async_copy(slab_ref.at[k], G.at[z, k], loc_sem.at[k])
 
-    q_own = pltpu.make_async_copy(q_ref, qb.at[0], loc_sem.at[K])
-    q_own.start()
-
-    @pl.loop(0, K)
-    def _(k):
-        local_slab(k).start()
-
-    qacc[...] = jnp.zeros_like(qacc)
     pl.semaphore_wait(barrier, 3 + has_r.astype(jnp.int32) + has_l.astype(jnp.int32))
 
     def column(block, core, k):
@@ -101,12 +93,16 @@
     def send_q():
         return remote(q_ref, qb.at[1], q_send, q_recv, sib)
 
-    def sum_right(dest, h):
-        return remote(RS.at[dest, h], RS.at[dest, h], r_send.at[dest, h], r_recv.at[dest, h], right)
-
-    def sum_left(dest, h):
+    def rows_of(slot, h, part):
+        return RS.at[slot, h] if part is None else RS.at[slot, h, pl.ds(part * (w // 2), w // 2)]
+
+    def sum_right(dest, h, part=None):
+        src = rows_of(dest, h, part)
+        return remote(src, src, r_send.at[dest, h], r_recv.at[dest, h], right)
+
+    def sum_left(dest, h, part=None):
         slot = jnp.where(dest == z - 1, n, dest)
-        return remote(RS.at[dest, h], RS.at[slot, h], r_send.at[dest, h], r_recv.at[slot, h], left)
+        return remote(rows_of(dest, h, part), rows_of(slot, h, part), r_send.at[dest, h], r_recv.at[slot, h], left)
 
     def arrived(slot, h):
         remote(RS.at[slot, h], RS.at[slot, h], r_send.at[0, 0], r_recv.at[slot, h], sib).wait_recv()
@@ -125,7 +121,11 @@
         def _():
             send_q().start()
 
+        local_slab(k).start()
         swap(z, k).start()
+
+    q_own = pltpu.make_async_copy(q_ref, qb.at[0], loc_sem.at[K])
+    q_own.start()
 
     @pl.loop(0, (n - 1) * K)
     def _(j):
@@ -139,6 +139,7 @@
         def _():
             swap(z - d, k).start()
 
+    qacc[...] = jnp.zeros_like(qacc)
     q_own.wait()
     send_q().wait_recv()
 
@@ -170,7 +171,7 @@
         grads = gs[...].reshape(2 * rows, w)
         both = qb[...].reshape(2 * rows, D)
         part = lax.dot_general(grads, both, (((0,), (0,)), ((), ())), preferred_element_type=F32)
-        PS[block, pl.ds(2 * k, 2)] = part.reshape(2, w // 2, D)
+        PS[block, k] = part
 
     def turn(i, at):
         near_far = jnp.where(i < H, 1, jnp.where(i < 2 * H, 2, jnp.where(i < 3 * H, 3, 1)))
@@ -187,24 +188,49 @@
         ok = ((at == 0) & near_ok) | ((at == 1) & mid_ok) | ((at == 2) & last_ok)
         return far, h, ok
 
+    def add(dest, h):
+        arrived(dest, h)
+        RS[dest, h] = (RS[dest, h].astype(F32) + PS[dest, h]).astype(BF16)
+
+    def sent(i):
+        for at, going_right in ((z, True), (zm, False)):
+            far, h, ok = turn(i - LAG, at)
+            dest = far if going_right else n - 1 - far
+
+            @pl.when(ok)
+            def _(dest=dest, h=h):
+                sum_right(dest, h).wait_send()
+
     def sums(i):
         for at, going_right in ((z, True), (zm, False)):
             far, h, ok = turn(i, at)
             dest = far if going_right else n - 1 - far
-
-            @pl.when(ok)
-            def _(at=at, h=h, dest=dest, going_right=going_right):
+            mid = 2 if going_right else n - 3
+            send = sum_right if going_right else sum_left
+            second = (at == 1) & (i == 3 * H + NEAR)
+
+            @pl.when(ok & jnp.logical_not(second))
+            def _(at=at, h=h, dest=dest, send=send):
                 @pl.when(at > 0)
                 def _():
-                    arrived(dest, h)
-                    RS[dest, h] = (RS[dest, h].astype(F32) + PS[dest, h]).astype(BF16)
+                    add(dest, h)
 
                 @pl.when(at == 0)
                 def _():
                     RS[dest, h] = PS[dest, h].astype(BF16)
 
-                (sum_right if going_right else sum_left)(dest, h).start()
-
+                send(dest, h).start()
+
+            @pl.when((at == 1) & (i == H + NEAR + MID))
+            def _(mid=mid, send=send):
+                add(mid, MID)
+                send(mid, MID, 0).start()
+
+            @pl.when(second)
+            def _(mid=mid, send=send):
+                send(mid, MID, 1).start()
+
+        sent(i)
         t = i - 3 * H
 
         @pl.when((t >= 0) & (t < H))
@@ -258,9 +284,7 @@
             def _():
                 tile(block, k)
 
-        @pl.loop(2 * j, 2 * j + 2)
-        def _(i):
-            sums(i)
+        sums(j)
 
     theirs = remote(qacc.at[1], qr, a_send, a_recv, sib)
 
@@ -275,44 +299,46 @@
     qacc[0] += qr[...]
     for h in range(2):
         over(0, h).start()
+    send_q().wait_send()
+
+    @pl.loop(0, n * K)
+    def _(j):
+        block, k = j // K, j % K
+        swap(block, k).wait_send()
+
+        @pl.when(has_r & (block <= z))
+        def _():
+            pass_right(block, k).wait_send()
+
+        @pl.when(has_l & (block >= z))
+        def _():
+            pass_left(block, k).wait_send()
+
     pl.loop(3 * H + 1, 3 * H + H // 2)(sums)
     for h in range(2):
         over(0, h).wait_recv()
         xr[0, h] += qacc[0, h * half : (h + 1) * half, :]
         over(1, h).start()
     pl.loop(3 * H + H // 2, 4 * H - 1)(sums)
+    theirs.wait_send()
+    for h in range(2):
+        over(0, h).wait_send()
     for h in range(2):
         over(1, h).wait_recv()
         qout[h * half : (h + 1) * half, :] = (xr[0, h] + xr[1, h]).astype(BF16)
     pl.loop(4 * H - 1, 4 * H)(sums)
 
     for h in range(2):
-        over(0, h).wait_send()
         over(1, h).wait_send()
-    theirs.wait_send()
-    send_q().wait_send()
-
-    @pl.loop(0, n * K)
-    def _(j):
-        block, k = j // K, j % K
-        swap(block, k).wait_send()
-
-        @pl.when(has_r & (block <= z))
-        def _():
-            pass_right(block, k).wait_send()
-
-        @pl.when(has_l & (block >= z))
-        def _():
-            pass_left(block, k).wait_send()
-
-        @pl.when(block != z)
-        def _():
-            sum_right(block, 2 * k).wait_send()
-            sum_right(block, 2 * k + 1).wait_send()
+
+    @pl.loop(4 * H, 4 * H + LAG)
+    def _(i):
+        sent(i)
 
 
 def copy_kernel(q_ref, s_ref, q_out, s_out, sem):
-    copies = [pltpu.make_async_copy(q_ref, q_out, sem.at[0]), pltpu.make_async_copy(s_ref, s_out, sem.at[1])]
+    copies = [pltpu.make_async_copy(q_ref, q_out, sem.at[0])]
+    copies.append(pltpu.make_async_copy(s_ref, s_out, sem.at[1]))
     for copy in copies:
         copy.start()
     for copy in copies:
@@ -328,7 +354,7 @@
         in_specs=[vmem, vmem],
         compiler_params=pltpu.CompilerParams(vmem_limit_bytes=2**20),
         out_specs=(hbm, hbm),
-        scratch_shapes=[pltpu.SemaphoreType.DMA((2,))],
+        scratch_shapes=[pltpu.SemaphoreType.DMA((slab_grad.shape[0] + 1,))],
     )(*(pltpu.with_memory_space_constraint(x, pltpu.VMEM) for x in (query_grad, slab_grad)))
 
 
@@ -344,15 +370,15 @@
         lambda *refs: line_kernel(n, win, *refs),
         out_shape=(
             pltpu.VMEM((rows, D), BF16),
-            pltpu.VMEM((2 * K, w // 2, D), BF16),
+            pltpu.VMEM((K, w, D), BF16),
             jax.ShapeDtypeStruct((n, K, rows, win), jnp.int32),
         ),
         in_specs=[hbm, hbm, hbm],
         out_specs=(vmem, vmem, hbm),
         scratch_shapes=[
             pltpu.VMEM((n, K, w, D), BF16),
-            pltpu.VMEM((n + 1, 2 * K, w // 2, D), BF16),
-            pltpu.VMEM((n, 2 * K, w // 2, D), F32),
+            pltpu.VMEM((n + 1, K, w, D), BF16),
+            pltpu.VMEM((n, K, w, D), F32),
             pltpu.VMEM((2, rows, D), BF16),
             pltpu.VMEM((2, rows, D), F32),
             pltpu.VMEM((2, rows, win), jnp.int32),
@@ -360,7 +386,7 @@
             pltpu.VMEM((rows, D), F32),
             pltpu.VMEM((2, 2, rows // 2, D), F32),
             dma((K + 1,)), dma, dma, dma((n, K)), dma((n, K)), dma((2,)),
-            dma((2, n, K)), dma((n, K)), dma((n, 2 * K)), dma((n + 1, 2 * K)), dma, dma, dma((2, 2)), dma((2, 2)),
+            dma((2, n, K)), dma((n, K)), dma((n, K)), dma((n + 1, K)), dma, dma, dma((2, 2)), dma((2, 2)),
         ],
         compiler_params=pltpu.CompilerParams(
             collective_id=0, has_side_effects=True, vmem_limit_bytes=58 * 2**20

time: 221 us -> 221 us (level)
  no operation moved by 1% of the time
where the time goes in v3:
time: 221 us; the launch traced here: 220 us
  Pallas kernels  220 us (100%)
    pallas_call x1, Pallas kernels, fused(): pl.pallas_call(lambda *refs: line_kernel(n, win, *refs), out_shape=(pltpu...  218 us

profile of v3, /device:TPU:0, one launch (start us, length us, event | category | flops | bytes accessed | tf_op | source)
XLA Modules:
  0.0 220.2 jit_solution(16536595337454187947)
XLA Ops:
  0.6 217.8 %shard_map.50 = (bf16[512,768]{1,0:T(8,128)(2,1)S(1)}, bf16[5,320,768]{2,1,0:T(8,128)(2,1)S(1)}, s32[4,5,512,384]{3,2,1,0:T(8,128)}) custom-call(bf16[512,768]{1,0:T(8,128)(2,1)} %refs_0_.1, bf16[5,320,768]{2,1,0:T(8,128)(2,1)} %bitcast.2, s32[512,12800]{1,0:T(8,128)} %refs_2_.1), custom_call_target="tpu_custom_call" | custom-call | flops 30198988800 | bytes 26214400 | tf_op jit(solution)/shard_map/pallas_call | solution.py:369
  218.4 1.8 shard_map.51

commit v4 on v3

--- a/solution.py
+++ b/solution.py
@@ -9,7 +9,7 @@
 MESH = pl.DeviceIdType.MESH
 F32, BF16 = jnp.float32, jnp.bfloat16
 PARTS = 5
-NEAR, MID, LAG = 2, 3, 5
+NEAR, MID, LAG, LEAD = 2, 3, 5, 2
 
 
 def plain(queries, slab, positives):
@@ -122,23 +122,26 @@
             send_q().start()
 
         local_slab(k).start()
-        swap(z, k).start()
 
     q_own = pltpu.make_async_copy(q_ref, qb.at[0], loc_sem.at[K])
     q_own.start()
 
-    @pl.loop(0, (n - 1) * K)
-    def _(j):
+    def swaps(j):
         d, k = j // K + 1, j % K
 
-        @pl.when(z + d < n)
+        @pl.when(j < K)
+        def _():
+            swap(z, k).start()
+
+        @pl.when((j < (n - 1) * K) & (z + d < n))
         def _():
             swap(z + d, k).start()
 
-        @pl.when(z - d >= 0)
+        @pl.when((j < (n - 1) * K) & (z - d >= 0))
         def _():
             swap(z - d, k).start()
 
+    pl.loop(0, LEAD)(swaps)
     qacc[...] = jnp.zeros_like(qacc)
     q_own.wait()
     send_q().wait_recv()
@@ -238,18 +241,27 @@
             @pl.when(has_l)
             def _():
                 arrived(z, t)
-                PS[z, t] += RS[z, t].astype(F32)
 
             @pl.when(has_r)
             def _():
                 arrived(n, t)
-                PS[z, t] += RS[n, t].astype(F32)
-
-            sout[t] = PS[z, t].astype(BF16)
+
+            @pl.when(has_l & has_r)
+            def _():
+                sout[t] = (PS[z, t] + RS[z, t].astype(F32) + RS[n, t].astype(F32)).astype(BF16)
+
+            @pl.when(has_l & jnp.logical_not(has_r))
+            def _():
+                sout[t] = (PS[z, t] + RS[z, t].astype(F32)).astype(BF16)
+
+            @pl.when(has_r & jnp.logical_not(has_l))
+            def _():
+                sout[t] = (PS[z, t] + RS[n, t].astype(F32)).astype(BF16)
 
     @pl.loop(0, (n - 1) * K)
     def _(j):
         d, k = j // K + 1, j % K
+        swaps(j + LEAD)
 
         @pl.when(j < K)
         def _():

time: 221 us -> 221 us (level)
  no operation moved by 1% of the time
where the time goes in v4:
time: 221 us; the launch traced here: 220 us
  Pallas kernels  219 us (99%)
    pallas_call x1, Pallas kernels, fused(): pl.pallas_call(lambda *refs: line_kernel(n, win, *refs), out_shape=(pltpu...  218 us

profile of v4, /device:TPU:0, one launch (start us, length us, event | category | flops | bytes accessed | tf_op | source)
XLA Modules:
  0.0 220.1 jit_solution(6266229814253654599)
XLA Ops:
  0.6 217.7 %shard_map.50 = (bf16[512,768]{1,0:T(8,128)(2,1)S(1)}, bf16[5,320,768]{2,1,0:T(8,128)(2,1)S(1)}, s32[4,5,512,384]{3,2,1,0:T(8,128)}) custom-call(bf16[512,768]{1,0:T(8,128)(2,1)} %refs_0_.1, bf16[5,320,768]{2,1,0:T(8,128)(2,1)} %bitcast.2, s32[512,12800]{1,0:T(8,128)} %refs_2_.1), custom_call_target="tpu_custom_call" | custom-call | flops 30198988800 | bytes 26214400 | tf_op jit(solution)/shard_map/pallas_call | solution.py:381
  218.4 1.8 shard_map.51

commit v5 on v4

--- a/solution.py
+++ b/solution.py
@@ -212,9 +212,9 @@
             send = sum_right if going_right else sum_left
             second = (at == 1) & (i == 3 * H + NEAR)
 
-            @pl.when(ok & jnp.logical_not(second))
+            @pl.when(ok & (at < 2) & jnp.logical_not(second))
             def _(at=at, h=h, dest=dest, send=send):
-                @pl.when(at > 0)
+                @pl.when(at == 1)
                 def _():
                     add(dest, h)
 
@@ -232,6 +232,16 @@
             @pl.when(second)
             def _(mid=mid, send=send):
                 send(mid, MID, 1).start()
+
+        for at, going_right in ((z, True), (zm, False)):
+            far, h, ok = turn(i, at)
+            dest = far if going_right else n - 1 - far
+            send = sum_right if going_right else sum_left
+
+            @pl.when(ok & (at == 2))
+            def _(h=h, dest=dest, send=send):
+                add(dest, h)
+                send(dest, h).start()
 
         sent(i)
         t = i - 3 * H

time: 221 us -> 221 us (level)
  no operation moved by 1% of the time
where the time goes in v5:
time: 221 us; the launch traced here: 220 us
  Pallas kernels  219 us (99%)
    pallas_call x1, Pallas kernels, fused(): pl.pallas_call(lambda *refs: line_kernel(n, win, *refs), out_shape=(pltpu...  218 us

profile of v5, /device:TPU:0, one launch (start us, length us, event | category | flops | bytes accessed | tf_op | source)
XLA Modules:
  0.0 220.1 jit_solution(18316978665153049320)
XLA Ops:
  0.6 217.7 %shard_map.50 = (bf16[512,768]{1,0:T(8,128)(2,1)S(1)}, bf16[5,320,768]{2,1,0:T(8,128)(2,1)S(1)}, s32[4,5,512,384]{3,2,1,0:T(8,128)}) custom-call(bf16[512,768]{1,0:T(8,128)(2,1)} %refs_0_.1, bf16[5,320,768]{2,1,0:T(8,128)(2,1)} %bitcast.2, s32[512,12800]{1,0:T(8,128)} %refs_2_.1), custom_call_target="tpu_custom_call" | custom-call | flops 30198988800 | bytes 26214400 | tf_op jit(solution)/shard_map/pallas_call | solution.py:391
  218.4 1.8 shard_map.51
